TPU v7x, 128 devices: a whole 4x4x4 slice. The times are simulated.
128 devices in a mesh: grid: 64 (over x, y, z_lo, core), col: 2 (over z_hi).
Axes of the slice: x: 4, y: 4, z: 4 (z_hi: 2, z_lo: 2; z = z_hi * 2 + z_lo), core: 2. Of those that a mesh axis runs over, the one named last changes fastest.
Arguments:
- orbitals: bfloat16 [884736, 256], P(('grid', 'col')), may hold values from -6 to 6
- points: int32 [1024], replicated, may hold values from 0 to 884735, as said below
- cinv: bfloat16 [1024, 256], replicated, may hold values from -0.1875 to 0.1875
Outputs:
- potential: bfloat16 [256, 884736], P(None, ('grid', 'col'))
- coupling: float32 [1024, 256], P(('grid', 'col'))
Inputs may be any that keep to these rules, and one draw needn't show every extreme that they name: `points`: 1024 distinct grid rows.
All inputs are finite; a program needn't handle non-finite values.
Results may differ from a plain program's by a relative error of at most 0.0046.
Values may be sent and summed in bfloat16 or wider, within the bound.
A program may use at most 192 MiB of HBM per device.

v0:
```python
import math
import jax
import jax.numpy as jnp
from jax import lax
from jax.sharding import PartitionSpec as P

NX = 96
screening = 0.25


def kernel_table(size):
    index = jnp.arange(size)
    wave = jnp.where(index < (size + 1) // 2, index, index - size).astype(jnp.float32) * (
        2.0 * math.pi / size
    )
    squared = wave[:, None, None] ** 2 + wave[None, :, None] ** 2 + wave[None, None, :] ** 2
    return jnp.where(squared > 0, 1.0 / (squared + screening), 0.0)


def along(table, values, axis):
    forms = {1: "kn,cnyz->ckyz", 2: "kn,cxnz->cxkz", 3: "kn,cxyn->cxyk"}
    return jnp.einsum(forms[axis], table, values, precision=lax.Precision.HIGHEST)


def screened_solve(field):
    size = field.shape[1]
    index = jnp.arange(size, dtype=jnp.int32)
    phase = index[:, None] * index[None, :] % size
    angle = phase.astype(jnp.float32) * (2.0 * math.pi / size)
    cos_table = jnp.cos(angle)
    sin_table = jnp.sin(angle)
    real_part = along(cos_table, field, 3)
    imag_part = -along(sin_table, field, 3)
    for axis in (2, 1):
        real_part, imag_part = (
            along(cos_table, real_part, axis) + along(sin_table, imag_part, axis),
            along(cos_table, imag_part, axis) - along(sin_table, real_part, axis),
        )
    weights = kernel_table(size)
    real_part = real_part * weights
    imag_part = imag_part * weights
    for axis in (1, 2):
        real_part, imag_part = (
            along(cos_table, real_part, axis) - along(sin_table, imag_part, axis),
            along(cos_table, imag_part, axis) + along(sin_table, real_part, axis),
        )
    result = along(cos_table, real_part, 3) - along(sin_table, imag_part, 3)
    return result / float(size**3)


def local(orbitals, points, cinv):
    ranks = lax.axis_size(("grid", "col"))
    local_rows = orbitals.shape[0]
    orbital_count = orbitals.shape[1]
    npoints = cinv.shape[0]
    columns = cinv.shape[1]
    per_rank = columns // ranks
    first_row = lax.axis_index(("grid", "col")) * local_rows
    offset = points - first_row
    inside = (offset >= 0) & (offset < local_rows)
    picked = jnp.take(orbitals, jnp.clip(offset, 0, local_rows - 1), axis=0)
    picked = jnp.where(inside[:, None], picked.astype(jnp.float32), 0.0)
    point_rows = lax.psum(picked, ("grid", "col")).astype(jnp.bfloat16)
    scale = 1.0 / math.sqrt(orbital_count)
    block_rows = math.gcd(local_rows, 1152)

    def pair_block(block):
        product = (
            lax.dot_general(
                block, point_rows, (((1,), (1,)), ((), ())), preferred_element_type=jnp.float32
            )
            * scale
        )
        return (product * product).astype(jnp.bfloat16)

    pairs = lax.map(
        pair_block, orbitals.reshape(local_rows // block_rows, block_rows, orbital_count)
    )
    pairs = pairs.reshape(local_rows, npoints)
    theta_cols = lax.dot_general(
        cinv, pairs, (((0,), (1,)), ((), ())), preferred_element_type=jnp.float32
    )
    fields = lax.all_to_all(theta_cols, ("grid", "col"), split_axis=0, concat_axis=1, tiled=True)
    fields = fields.reshape(per_rank, NX, NX, NX)
    potentials = screened_solve(fields).astype(jnp.bfloat16).reshape(per_rank, NX * NX * NX)
    rows_back = lax.all_to_all(potentials, ("grid", "col"), split_axis=1, concat_axis=0, tiled=True)
    factor = math.sqrt(npoints) / float(NX**3)
    coupling = lax.psum_scatter(
        lax.dot_general(
            pairs, rows_back, (((0,), (1,)), ((), ())), preferred_element_type=jnp.float32
        )
        * factor,
        ("grid", "col"),
        scatter_dimension=0,
        tiled=True,
    )
    return (rows_back, coupling)


def solution(mesh):
    in_specs = (P(("grid", "col"), None), P(), P())
    out_specs = (P(None, ("grid", "col")), P(("grid", "col"), None))
    return jax.shard_map(local, mesh=mesh, in_specs=in_specs, out_specs=out_specs, check_vma=False)
```

profile of v0, /device:TPU:0, one launch (start us, length us, event | category | flops | bytes accessed | tf_op | source)
XLA Modules:
  0.0 1324.5 jit_solution(9655108853187020111)
XLA Ops:
  7.2 0.8 compare_and_fusion.1
  7.9 0.7 fusion.144
  8.6 5.9 gather_fusion
  14.9 74.1 %all-reduce.1 = bf16[1024,256]{1,0:T(8,128)(2,1)S(1)} all-reduce(f32[1024,256]{1,0:T(8,128)S(1)} %convert_select_fusion), channel_id=1, replica_groups=mesh['grid'=64,'col'=2] {'grid','col'}, use_global_device_ids=true, to_apply=%region_0.1 | all-reduce | flops 262144 | bytes 1572864 | tf_op jit(solution)/shard_map/psum | solution.py:63
  89.0 19.9 %while.10 = (s32[]{:T(128)}, bf16[6,1152,1024]{2,1,0:T(8,128)(2,1)}, bf16[6,1152,256]{2,1,0:T(8,128)(2,1)}, bf16[1024,256]{1,0:T(8,128)(2,1)S(1)}, s32[]{:T(128)}) while((s32[]{:T(128)}, bf16[6,1152,1024]{2,1,0:T(8,128)(2,1)}, bf16[6,1152,256]{2,1,0:T(8,128)(2,1)}, bf16[1024,256]{1,0:T(8,128)(2,1)S(1)}, s32[]{:T(128)}) %tuple.28), condition=%wide.region_2.3_spmd, body=%wide.region_1.2_spmd.sunk | while | flops 607518720 | bytes 3474501 | solution.py:76
  89.0 3.3 fusion.234
  92.3 3.3 fusion.234
  95.7 3.3 fusion.234
  99.0 3.4 fusion.234
  102.3 3.3 fusion.234
  105.6 3.3 fusion.234
  109.0 11.7 convolution_bitcast_fusion
  120.7 9.1 all_to_all.26
  129.8 6.9 all-to-all-start
  137.1 3.1 fusion.18
  140.1 81.1 %all-to-all-done = f32[128,2,6912]{2,1,0:T(2,128)} async-done(((f32[128,2,6912]{2,1,0:T(2,128)}), f32[128,2,6912]{2,1,0:T(2,128)}, u32[]{:S(2)}, u32[]{:S(2)}) %all-to-all-start) | async-done | bytes 7077920 | tf_op jit(solution)/shard_map/all_to_all | solution.py:83
  221.2 6.4 copy.15
  227.6 10.6 reshape.103
  238.2 11.3 fusion.39
  249.5 21.2 %fusion.57 = f32[2,96,96,96]{2,3,1,0:T(8,128)S(1)} fusion(f32[2,96,96,96]{3,2,1,0:T(8,128)S(1)} %copy-done.6), kind=kOutput, calls=%fused_computation.66 | convolution fusion | flops 2038514688 | bytes 14155776 | tf_op jit(solution)/shard_map/kn,cxyn->cxyk/dot_general | solution.py:22
  270.7 8.8 fusion.55
  279.5 10.5 fusion.36
  290.0 19.2 %subtract_bitcast_fusion.1 = f32[2,96,96,96]{2,3,1,0:T(8,128)} fusion(f32[2,96,96,96]{3,2,1,0:T(8,128)} %fusion.36, f32[2,96,96,96]{3,2,1,0:T(8,128)S(1)} %fusion.39), kind=kOutput, calls=%fused_computation.21 | convolution fusion | flops 2042053632 | bytes 21233664 | tf_op jit(solution)/shard_map/kn,cxnz->cxkz/dot_general | solution.py:22
  309.2 17.8 %add_bitcast_fusion.1 = f32[2,96,96,96]{2,3,1,0:T(8,128)} fusion(f32[2,96,96,96]{3,2,1,0:T(8,128)S(1)} %fusion.55, f32[2,96,96,96]{3,2,1,0:T(8,128)S(1)} %fusion.39), kind=kOutput, calls=%fused_computation.22 | convolution fusion | flops 2042053632 | bytes 21233664 | tf_op jit(solution)/shard_map/kn,cxnz->cxkz/dot_general | solution.py:22
  326.9 12.4 copy.18
  339.3 12.4 copy.21
  351.7 13.4 %fusion.48 = f32[2,96,96,96]{3,2,1,0:T(8,128)} fusion(f32[2,96,96,96]{1,3,2,0:T(8,128)} %copy.21), kind=kOutput, calls=%fused_computation.57 | convolution fusion | flops 2038514688 | bytes 14155776 | tf_op jit(solution)/shard_map/kn,cnyz->ckyz/dot_general | solution.py:22
  365.1 10.2 fusion.53
  375.3 11.3 bitcast_multiply_fusion
  386.6 15.4 %bitcast_multiply_fusion.1 = f32[2,96,96,96]{1,3,2,0:T(8,128)S(1)} fusion(f32[2,96,96,96]{3,2,1,0:T(8,128)} %fusion.53, f32[96,96,96]{0,2,1:T(8,128)S(1)} %bitcast.109, f32[2,96,96,96]{1,3,2,0:T(8,128)} %copy.21), kind=kOutput, calls=%fused_computation.15 | convolution fusion | flops 2042053632 | bytes 24772608 | tf_op jit(solution)/shard_map/kn,cnyz->ckyz/dot_general | solution.py:22
  402.0 10.3 fusion.50
  412.3 8.8 fusion.44
  421.1 10.6 add_bitcast_fusion
  431.7 12.4 copy.31
  444.1 26.4 %fusion.41 = f32[2,96,96,96]{2,3,1,0:T(8,128)} fusion(f32[2,96,96,96]{2,3,1,0:T(8,128)} %copy.31), kind=kOutput, calls=%fused_computation.50 | convolution fusion | flops 2038514688 | bytes 14155776 | tf_op jit(solution)/shard_map/kn,cxnz->cxkz/dot_general | solution.py:22
  470.6 23.6 %fusion.30 = f32[2,96,96,96]{2,3,1,0:T(8,128)} fusion(f32[2,96,96,96]{2,3,1,0:T(8,128)S(1)} %copy-done.3), kind=kOutput, calls=%fused_computation.39 | convolution fusion | flops 2038514688 | bytes 14155776 | tf_op jit(solution)/shard_map/kn,cxnz->cxkz/dot_general | solution.py:22
  494.3 10.6 subtract_bitcast_fusion
  504.8 12.5 copy.30
  517.4 24.6 %fusion.28 = f32[2,96,96,96]{2,3,1,0:T(8,128)S(1)} fusion(f32[2,96,96,96]{2,3,1,0:T(8,128)} %copy.30), kind=kOutput, calls=%fused_computation.37 | convolution fusion | flops 2038514688 | bytes 14155776 | tf_op jit(solution)/shard_map/kn,cxnz->cxkz/dot_general | solution.py:22
  542.0 23.4 %fusion.46 = f32[2,96,96,96]{2,3,1,0:T(8,128)} fusion(f32[2,96,96,96]{2,3,1,0:T(8,128)S(1)} %copy-done.4), kind=kOutput, calls=%fused_computation.55 | convolution fusion | flops 2038514688 | bytes 14155776 | tf_op jit(solution)/shard_map/kn,cxnz->cxkz/dot_general | solution.py:22
  565.4 10.2 fusion.7
  575.6 15.9 %multiply_convert_fusion = bf16[2,96,96,96]{3,2,1,0:T(8,128)(2,1)} fusion(f32[2,96,96,96]{3,2,1,0:T(8,128)} %fusion.7, f32[2,96,96,96]{2,3,1,0:T(8,128)} %fusion.46, f32[2,96,96,96]{2,3,1,0:T(8,128)} %fusion.30), kind=kOutput, calls=%fused_computation.16 | convolution fusion | flops 2045592576 | bytes 24772608 | tf_op jit(solution)/shard_map/kn,cxyn->cxyk/dot_general | solution.py:22
  591.5 7.8 all_to_all.29
  599.3 5.6 copy.24
  604.9 55.8 %all_to_all.35 = bf16[2,128,6912]{2,0,1:T(2,128)(2,1)} all-to-all(bf16[2,128,6912]{2,0,1:T(2,128)(2,1)S(1)} %copy.24), channel_id=1, replica_groups=mesh['grid'=64,'col'=2] {'grid','col'}, dimensions={1} | all-to-all | bytes 7077888 | tf_op jit(solution)/shard_map/all_to_all | solution.py:86
  660.7 8.3 all_to_all.32
  669.0 10.9 convolution_multiply_fusion.1
  679.9 637.2 %reduce-scatter.2.cloned.1.call-done = f32[8,256]{1,0:T(8,128)} async-done(((f32[1024,256]{1,0:T(8,128)}), f32[8,256]{1,0:T(8,128)}) %reduce-scatter.2.cloned.1.call-update) | async-done | bytes 8208 | tf_op jit(solution)/shard_map/reduce_scatter | solution.py:88
  (46 shorter events, 0.8 us)
Async XLA Ops:
  7.2 101.8 %copy-start = (bf16[1024,256]{1,0:T(8,128)(2,1)S(1)}, bf16[1024,256]{1,0:T(8,128)(2,1)}, u32[]{:S(2)}) copy-start(bf16[1024,256]{1,0:T(8,128)(2,1)} %param.7) | copy-start | bytes 1572868
  129.8 91.4 %all-to-all-start = ((f32[128,2,6912]{2,1,0:T(2,128)}), f32[128,2,6912]{2,1,0:T(2,128)}, u32[]{:S(2)}, u32[]{:S(2)}) async-start(f32[128,2,6912]{2,1,0:T(2,128)} %all_to_all.26), calls=%async_computation | async-start | bytes 14155776 | tf_op jit(solution)/shard_map/all_to_all | solution.py:83
  136.7 1180.5 %reduce-scatter.2.cloned.1.call-start = ((), (), s32[]{:S(2)}) async-start(), calls=%async_computation.3 | async-start | bytes 1056768 | tf_op jit(solution)/shard_map/reduce_scatter | solution.py:88
  238.2 11.3 copy-start.6
  351.7 13.4 %copy-start.5 = (f32[2,96,96,96]{1,3,2,0:T(8,128)S(1)}, f32[2,96,96,96]{1,3,2,0:T(8,128)}, u32[]{:S(2)}) copy-start(f32[2,96,96,96]{1,3,2,0:T(8,128)} %copy.18) | copy-start | bytes 21233668
  351.7 23.6 %slice-start = ((s8[4718592]{0:T(1024)(128)(4,1)}), s8[4194304]{0:T(1024)(128)(4,1)S(1)}, s32[]{:S(2)}) async-start(s8[4718592]{0:T(1024)(128)(4,1)} %bitcast.108), calls=%async_computation.4 | async-start | bytes 8388608
  365.1 10.2 slice-start.1
  386.6 25.7 %copy-start.2 = (f32[2,96,96,96]{1,3,2,0:T(8,128)}, f32[2,96,96,96]{1,3,2,0:T(8,128)S(1)}, u32[]{:S(2)}) copy-start(f32[2,96,96,96]{1,3,2,0:T(8,128)S(1)} %bitcast_multiply_fusion) | copy-start | bytes 21233668
  444.1 26.4 %copy-start.3 = (f32[2,96,96,96]{2,3,1,0:T(8,128)S(1)}, f32[2,96,96,96]{2,3,1,0:T(8,128)}, u32[]{:S(2)}) copy-start(f32[2,96,96,96]{2,3,1,0:T(8,128)} %copy.31) | copy-start | bytes 21233668
  444.1 50.1 %slice-start.2 = ((s8[9437184]{0:T(1024)(128)(4,1)}), s8[4194304]{0:T(1024)(128)(4,1)S(1)}, s32[]{:S(2)}) async-start(s8[9437184]{0:T(1024)(128)(4,1)} %bitcast.110), calls=%async_computation.6 | async-start | bytes 8388608
  444.1 50.1 %slice-start.3 = ((s8[9437184]{0:T(1024)(128)(4,1)}), s8[4194304]{0:T(1024)(128)(4,1)S(1)}, s32[]{:S(2)}) async-start(s8[9437184]{0:T(1024)(128)(4,1)} %bitcast.110), calls=%async_computation.7 | async-start | bytes 8388608
  444.1 50.1 %slice-start.5 = ((s8[9437184]{0:T(1024)(128)(4,1)}), s8[4194304]{0:T(1024)(128)(4,1)S(1)}, s32[]{:S(2)}) async-start(s8[9437184]{0:T(1024)(128)(4,1)} %bitcast.112), calls=%async_computation.9 | async-start | bytes 8388608
  444.1 50.1 %slice-start.6 = ((s8[9437184]{0:T(1024)(128)(4,1)}), s8[4194304]{0:T(1024)(128)(4,1)S(1)}, s32[]{:S(2)}) async-start(s8[9437184]{0:T(1024)(128)(4,1)} %bitcast.112), calls=%async_computation.10 | async-start | bytes 8388608
  470.6 23.7 %slice-start.4 = ((s8[9437184]{0:T(1024)(128)(4,1)}), s8[1048576]{0:T(1024)(128)(4,1)S(1)}, s32[]{:S(2)}) async-start(s8[9437184]{0:T(1024)(128)(4,1)} %bitcast.110), calls=%async_computation.8 | async-start | bytes 2097152
  470.6 23.7 %slice-start.7 = ((s8[9437184]{0:T(1024)(128)(4,1)}), s8[1048576]{0:T(1024)(128)(4,1)S(1)}, s32[]{:S(2)}) async-start(s8[9437184]{0:T(1024)(128)(4,1)} %bitcast.112), calls=%async_computation.11 | async-start | bytes 2097152
  517.4 24.6 %copy-start.4 = (f32[2,96,96,96]{2,3,1,0:T(8,128)S(1)}, f32[2,96,96,96]{2,3,1,0:T(8,128)}, u32[]{:S(2)}) copy-start(f32[2,96,96,96]{2,3,1,0:T(8,128)} %copy.30) | copy-start | bytes 21233668
  517.4 48.0 %slice-start.8 = ((s8[9437184]{0:T(1024)(128)(4,1)}), s8[4194304]{0:T(1024)(128)(4,1)S(1)}, s32[]{:S(2)}) async-start(s8[9437184]{0:T(1024)(128)(4,1)} %bitcast.114), calls=%async_computation.12 | async-start | bytes 8388608
  517.4 48.0 %slice-start.9 = ((s8[9437184]{0:T(1024)(128)(4,1)}), s8[4194304]{0:T(1024)(128)(4,1)S(1)}, s32[]{:S(2)}) async-start(s8[9437184]{0:T(1024)(128)(4,1)} %bitcast.114), calls=%async_computation.13 | async-start | bytes 8388608
  542.0 23.4 %slice-start.10 = ((s8[9437184]{0:T(1024)(128)(4,1)}), s8[1048576]{0:T(1024)(128)(4,1)S(1)}, s32[]{:S(2)}) async-start(s8[9437184]{0:T(1024)(128)(4,1)} %bitcast.114), calls=%async_computation.14 | async-start | bytes 2097152
  660.7 656.4 %copy-start.1 = (bf16[1024,256]{1,0:T(8,128)(2,1)S(1)}, bf16[1024,256]{1,0:T(8,128)(2,1)}, u32[]{:S(2)}) copy-start(bf16[1024,256]{1,0:T(8,128)(2,1)} %param.7) | copy-start | bytes 1572868
Sparse Core Ops, SparseCore 0:
  680.1 637.0 reduce-scatter.1
where the time goes:
time: 1330 us; the launch traced here: 1320 us
  waiting for transfers between devices  718 us (54%)
  matrix products  346 us (26%)
  blocking collectives  130 us (10%)
  local copies, waits for them, and re-layouts  103 us (8%)
  between operations  14.8 us (1%)
    reduce_scatter x1, waiting for transfers between devices, local(): lax.psum_scatter(lax.dot_general(pairs, rows_back, (((0,), (1,)), ((), ()...  637 us
    dot_general x20, matrix products, along(): jnp.einsum(forms[axis], table, values, precision=lax.Precision.HIGHEST)  303 us
    all_to_all x1, waiting for transfers between devices, local(): lax.all_to_all(theta_cols, ('grid', 'col'), split_axis=0, concat_axis=1,...  81.1 us
    psum x1, blocking collectives, local(): point_rows = lax.psum(picked, ('grid', 'col')).astype(jnp.bfloat16)  74.1 us
    all_to_all x1, blocking collectives, local(): lax.all_to_all(potentials, ('grid', 'col'), split_axis=1, concat_axis=0,...  55.8 us
  transfers between devices with their start and end apart: 2, of which 2 were waited for; matrix products, arithmetic and copies ran while one was open for 0% of the time, Pallas kernels for 0%

commit v1 on v0

--- a/solution.py
+++ b/solution.py
@@ -60,7 +60,7 @@
     inside = (offset >= 0) & (offset < local_rows)
     picked = jnp.take(orbitals, jnp.clip(offset, 0, local_rows - 1), axis=0)
     picked = jnp.where(inside[:, None], picked.astype(jnp.float32), 0.0)
-    point_rows = lax.psum(picked, ("grid", "col")).astype(jnp.bfloat16)
+    point_rows = lax.psum(lax.psum(picked, "col"), "grid").astype(jnp.bfloat16)
     scale = 1.0 / math.sqrt(orbital_count)
     block_rows = math.gcd(local_rows, 1152)
 

time: 1330 us -> 1600 us (1.20)
  blocking collectives: 130 us -> 344 us
  waiting for transfers between devices: 718 us -> 769 us
    psum x1, blocking collectives: 74.1 us -> 289 us  [local(): point_rows = lax.psum(lax.psum(picked, 'col'), 'grid').astype(jnp.bfloat16)]
    psum x0 -> x1, waiting for transfers between devices: none -> 50.8 us  [local(): point_rows = lax.psum(lax.psum(picked, 'col'), 'grid').astype(jnp.bfloat16)]
  transfers between devices with their start and end apart: 2 -> 3, of which waited for: 2 -> 3; matrix products, arithmetic and copies ran while one was open for 0% -> 0% of each run, Pallas kernels for 0% -> 0%
where the time goes in v1:
time: 1600 us; the launch traced here: 1590 us
  waiting for transfers between devices  769 us (48%)
  matrix products  346 us (22%)
  blocking collectives  344 us (22%)
  local copies, waits for them, and re-layouts  103 us (6%)
    reduce_scatter x1, waiting for transfers between devices, local(): lax.psum_scatter(lax.dot_general(pairs, rows_back, (((0,), (1,)), ((), ()...  637 us
    dot_general x20, matrix products, along(): jnp.einsum(forms[axis], table, values, precision=lax.Precision.HIGHEST)  303 us
    psum x1, blocking collectives, local(): point_rows = lax.psum(lax.psum(picked, 'col'), 'grid').astype(jnp.bfloat16)  289 us
    all_to_all x1, waiting for transfers between devices, local(): lax.all_to_all(theta_cols, ('grid', 'col'), split_axis=0, concat_axis=1,...  81 us
    all_to_all x1, blocking collectives, local(): lax.all_to_all(potentials, ('grid', 'col'), split_axis=1, concat_axis=0,...  55.9 us
    psum x1, waiting for transfers between devices, local(): point_rows = lax.psum(lax.psum(picked, 'col'), 'grid').astype(jnp.bfloat16)  50.8 us
  transfers between devices with their start and end apart: 3, of which 3 were waited for; matrix products, arithmetic and copies ran while one was open for 0% of the time, Pallas kernels for 0%

profile of v1, /device:TPU:0, one launch (start us, length us, event | category | flops | bytes accessed | tf_op | source)
XLA Modules:
  0.0 1589.7 jit_solution(13767758844243913573)
XLA Ops:
  8.7 5.9 gather_fusion
  14.6 1.3 convert_select_fusion
  15.9 50.8 %all-reduce.3.cloned.1.call-done = f32[1024,256]{1,0:T(8,128)} async-done(((f32[1024,256]{1,0:T(8,128)}), f32[1024,256]{1,0:T(8,128)}) %all-reduce.3.cloned.1.call-update) | async-done | bytes 1048592 | tf_op jit(solution)/shard_map/psum | solution.py:63
  66.8 288.5 %all-reduce.4 = bf16[1024,256]{1,0:T(8,128)(2,1)S(1)} all-reduce(f32[1024,256]{1,0:T(8,128)} %all-reduce.3.cloned.1.call-done), channel_id=1, replica_groups=mesh['grid'=64,'col'=2] {'grid'}, use_global_device_ids=true, to_apply=%region_1.2 | all-reduce | flops 262144 | bytes 1572864 | tf_op jit(solution)/shard_map/psum | solution.py:63
  355.3 19.9 %while.10 = (s32[]{:T(128)}, bf16[6,1152,1024]{2,1,0:T(8,128)(2,1)}, bf16[6,1152,256]{2,1,0:T(8,128)(2,1)}, bf16[1024,256]{1,0:T(8,128)(2,1)S(1)}, s32[]{:T(128)}) while((s32[]{:T(128)}, bf16[6,1152,1024]{2,1,0:T(8,128)(2,1)}, bf16[6,1152,256]{2,1,0:T(8,128)(2,1)}, bf16[1024,256]{1,0:T(8,128)(2,1)S(1)}, s32[]{:T(128)}) %tuple.30), condition=%wide.region_3.4_spmd, body=%wide.region_2.3_spmd.sunk | while | flops 607518720 | bytes 3474501 | solution.py:76
  355.3 3.3 fusion.234
  358.6 3.3 fusion.234
  362.0 3.3 fusion.234
  365.3 3.4 fusion.234
  368.6 3.3 fusion.234
  371.9 3.3 fusion.234
  375.3 11.7 convolution_bitcast_fusion
  387.0 9.1 all_to_all.26
  396.1 5.8 all-to-all-start
  402.3 3.1 fusion.18
  405.3 81.0 %all-to-all-done = f32[128,2,6912]{2,1,0:T(2,128)} async-done(((f32[128,2,6912]{2,1,0:T(2,128)}), f32[128,2,6912]{2,1,0:T(2,128)}, u32[]{:S(2)}, u32[]{:S(2)}) %all-to-all-start) | async-done | bytes 7077920 | tf_op jit(solution)/shard_map/all_to_all | solution.py:83
  486.3 6.4 copy.15
  492.7 10.6 reshape.103
  503.3 11.3 fusion.39
  514.6 21.2 %fusion.57 = f32[2,96,96,96]{2,3,1,0:T(8,128)S(1)} fusion(f32[2,96,96,96]{3,2,1,0:T(8,128)S(1)} %copy-done.6), kind=kOutput, calls=%fused_computation.66 | convolution fusion | flops 2038514688 | bytes 14155776 | tf_op jit(solution)/shard_map/kn,cxyn->cxyk/dot_general | solution.py:22
  535.8 8.8 fusion.55
  544.6 10.5 fusion.36
  555.1 19.2 %subtract_bitcast_fusion.1 = f32[2,96,96,96]{2,3,1,0:T(8,128)} fusion(f32[2,96,96,96]{3,2,1,0:T(8,128)} %fusion.36, f32[2,96,96,96]{3,2,1,0:T(8,128)S(1)} %fusion.39), kind=kOutput, calls=%fused_computation.21 | convolution fusion | flops 2042053632 | bytes 21233664 | tf_op jit(solution)/shard_map/kn,cxnz->cxkz/dot_general | solution.py:22
  574.3 17.8 %add_bitcast_fusion.1 = f32[2,96,96,96]{2,3,1,0:T(8,128)} fusion(f32[2,96,96,96]{3,2,1,0:T(8,128)S(1)} %fusion.55, f32[2,96,96,96]{3,2,1,0:T(8,128)S(1)} %fusion.39), kind=kOutput, calls=%fused_computation.22 | convolution fusion | flops 2042053632 | bytes 21233664 | tf_op jit(solution)/shard_map/kn,cxnz->cxkz/dot_general | solution.py:22
  592.0 12.4 copy.18
  604.4 12.4 copy.21
  616.8 13.4 fusion.48
  630.2 10.2 fusion.53
  640.4 11.3 bitcast_multiply_fusion
  651.7 15.4 bitcast_multiply_fusion.1
  667.1 10.3 fusion.50
  677.4 8.8 fusion.44
  686.2 10.6 add_bitcast_fusion
  696.8 12.4 copy.31
  709.2 26.4 %fusion.41 = f32[2,96,96,96]{2,3,1,0:T(8,128)} fusion(f32[2,96,96,96]{2,3,1,0:T(8,128)} %copy.31), kind=kOutput, calls=%fused_computation.50 | convolution fusion | flops 2038514688 | bytes 14155776 | tf_op jit(solution)/shard_map/kn,cxnz->cxkz/dot_general | solution.py:22
  735.7 23.6 %fusion.30 = f32[2,96,96,96]{2,3,1,0:T(8,128)} fusion(f32[2,96,96,96]{2,3,1,0:T(8,128)S(1)} %copy-done.3), kind=kOutput, calls=%fused_computation.39 | convolution fusion | flops 2038514688 | bytes 14155776 | tf_op jit(solution)/shard_map/kn,cxnz->cxkz/dot_general | solution.py:22
  759.4 10.6 subtract_bitcast_fusion
  769.9 12.5 copy.30
  782.5 24.6 %fusion.28 = f32[2,96,96,96]{2,3,1,0:T(8,128)S(1)} fusion(f32[2,96,96,96]{2,3,1,0:T(8,128)} %copy.30), kind=kOutput, calls=%fused_computation.37 | convolution fusion | flops 2038514688 | bytes 14155776 | tf_op jit(solution)/shard_map/kn,cxnz->cxkz/dot_general | solution.py:22
  807.1 23.4 %fusion.46 = f32[2,96,96,96]{2,3,1,0:T(8,128)} fusion(f32[2,96,96,96]{2,3,1,0:T(8,128)S(1)} %copy-done.4), kind=kOutput, calls=%fused_computation.55 | convolution fusion | flops 2038514688 | bytes 14155776 | tf_op jit(solution)/shard_map/kn,cxnz->cxkz/dot_general | solution.py:22
  830.5 10.2 fusion.7
  840.7 15.9 %multiply_convert_fusion = bf16[2,96,96,96]{3,2,1,0:T(8,128)(2,1)} fusion(f32[2,96,96,96]{3,2,1,0:T(8,128)} %fusion.7, f32[2,96,96,96]{2,3,1,0:T(8,128)} %fusion.46, f32[2,96,96,96]{2,3,1,0:T(8,128)} %fusion.30), kind=kOutput, calls=%fused_computation.16 | convolution fusion | flops 2045592576 | bytes 24772608 | tf_op jit(solution)/shard_map/kn,cxyn->cxyk/dot_general | solution.py:22
  856.6 7.8 all_to_all.29
  864.4 5.6 copy.24
  870.0 55.9 %all_to_all.35 = bf16[2,128,6912]{2,0,1:T(2,128)(2,1)} all-to-all(bf16[2,128,6912]{2,0,1:T(2,128)(2,1)S(1)} %copy.24), channel_id=1, replica_groups=mesh['grid'=64,'col'=2] {'grid','col'}, dimensions={1} | all-to-all | bytes 7077888 | tf_op jit(solution)/shard_map/all_to_all | solution.py:86
  926.0 8.3 all_to_all.32
  934.3 10.9 convolution_multiply_fusion.1
  945.1 637.2 %reduce-scatter.2.cloned.1.call-done = f32[8,256]{1,0:T(8,128)} async-done(((f32[1024,256]{1,0:T(8,128)}), f32[8,256]{1,0:T(8,128)}) %reduce-scatter.2.cloned.1.call-update) | async-done | bytes 8208 | tf_op jit(solution)/shard_map/reduce_scatter | solution.py:88
  (49 shorter events, 1.9 us)
Async XLA Ops:
  7.2 368.1 %copy-start = (bf16[1024,256]{1,0:T(8,128)(2,1)S(1)}, bf16[1024,256]{1,0:T(8,128)(2,1)}, u32[]{:S(2)}) copy-start(bf16[1024,256]{1,0:T(8,128)(2,1)} %param.7) | copy-start | bytes 1572868
  7.2 59.6 %all-reduce.3.cloned.1.call-start = ((), (), s32[]{:S(2)}) async-start(), calls=%async_computation.3 | async-start | bytes 2097152 | tf_op jit(solution)/shard_map/psum | solution.py:63
  396.1 90.2 %all-to-all-start = ((f32[128,2,6912]{2,1,0:T(2,128)}), f32[128,2,6912]{2,1,0:T(2,128)}, u32[]{:S(2)}, u32[]{:S(2)}) async-start(f32[128,2,6912]{2,1,0:T(2,128)} %all_to_all.26), calls=%async_computation | async-start | bytes 14155776 | tf_op jit(solution)/shard_map/all_to_all | solution.py:83
  401.9 1180.5 %reduce-scatter.2.cloned.1.call-start = ((), (), s32[]{:S(2)}) async-start(), calls=%async_computation.4 | async-start | bytes 1056768 | tf_op jit(solution)/shard_map/reduce_scatter | solution.py:88
  503.3 11.3 copy-start.6
  616.8 13.4 copy-start.5
  616.8 23.6 %slice-start = ((s8[4718592]{0:T(1024)(128)(4,1)}), s8[4194304]{0:T(1024)(128)(4,1)S(1)}, s32[]{:S(2)}) async-start(s8[4718592]{0:T(1024)(128)(4,1)} %bitcast.108), calls=%async_computation.5 | async-start | bytes 8388608
  630.2 10.2 slice-start.1
  651.7 25.7 %copy-start.2 = (f32[2,96,96,96]{1,3,2,0:T(8,128)}, f32[2,96,96,96]{1,3,2,0:T(8,128)S(1)}, u32[]{:S(2)}) copy-start(f32[2,96,96,96]{1,3,2,0:T(8,128)S(1)} %bitcast_multiply_fusion) | copy-start | bytes 21233668
  709.2 26.4 %copy-start.3 = (f32[2,96,96,96]{2,3,1,0:T(8,128)S(1)}, f32[2,96,96,96]{2,3,1,0:T(8,128)}, u32[]{:S(2)}) copy-start(f32[2,96,96,96]{2,3,1,0:T(8,128)} %copy.31) | copy-start | bytes 21233668
  709.2 50.1 %slice-start.2 = ((s8[9437184]{0:T(1024)(128)(4,1)}), s8[4194304]{0:T(1024)(128)(4,1)S(1)}, s32[]{:S(2)}) async-start(s8[9437184]{0:T(1024)(128)(4,1)} %bitcast.110), calls=%async_computation.7 | async-start | bytes 8388608
  709.2 50.1 %slice-start.3 = ((s8[9437184]{0:T(1024)(128)(4,1)}), s8[4194304]{0:T(1024)(128)(4,1)S(1)}, s32[]{:S(2)}) async-start(s8[9437184]{0:T(1024)(128)(4,1)} %bitcast.110), calls=%async_computation.8 | async-start | bytes 8388608
  709.2 50.1 %slice-start.5 = ((s8[9437184]{0:T(1024)(128)(4,1)}), s8[4194304]{0:T(1024)(128)(4,1)S(1)}, s32[]{:S(2)}) async-start(s8[9437184]{0:T(1024)(128)(4,1)} %bitcast.112), calls=%async_computation.10 | async-start | bytes 8388608
  709.2 50.1 %slice-start.6 = ((s8[9437184]{0:T(1024)(128)(4,1)}), s8[4194304]{0:T(1024)(128)(4,1)S(1)}, s32[]{:S(2)}) async-start(s8[9437184]{0:T(1024)(128)(4,1)} %bitcast.112), calls=%async_computation.11 | async-start | bytes 8388608
  735.7 23.7 %slice-start.4 = ((s8[9437184]{0:T(1024)(128)(4,1)}), s8[1048576]{0:T(1024)(128)(4,1)S(1)}, s32[]{:S(2)}) async-start(s8[9437184]{0:T(1024)(128)(4,1)} %bitcast.110), calls=%async_computation.9 | async-start | bytes 2097152
  735.7 23.7 %slice-start.7 = ((s8[9437184]{0:T(1024)(128)(4,1)}), s8[1048576]{0:T(1024)(128)(4,1)S(1)}, s32[]{:S(2)}) async-start(s8[9437184]{0:T(1024)(128)(4,1)} %bitcast.112), calls=%async_computation.12 | async-start | bytes 2097152
  782.5 24.6 %copy-start.4 = (f32[2,96,96,96]{2,3,1,0:T(8,128)S(1)}, f32[2,96,96,96]{2,3,1,0:T(8,128)}, u32[]{:S(2)}) copy-start(f32[2,96,96,96]{2,3,1,0:T(8,128)} %copy.30) | copy-start | bytes 21233668
  782.5 48.0 %slice-start.8 = ((s8[9437184]{0:T(1024)(128)(4,1)}), s8[4194304]{0:T(1024)(128)(4,1)S(1)}, s32[]{:S(2)}) async-start(s8[9437184]{0:T(1024)(128)(4,1)} %bitcast.114), calls=%async_computation.13 | async-start | bytes 8388608
  782.5 48.0 %slice-start.9 = ((s8[9437184]{0:T(1024)(128)(4,1)}), s8[4194304]{0:T(1024)(128)(4,1)S(1)}, s32[]{:S(2)}) async-start(s8[9437184]{0:T(1024)(128)(4,1)} %bitcast.114), calls=%async_computation.14 | async-start | bytes 8388608
  807.1 23.4 %slice-start.10 = ((s8[9437184]{0:T(1024)(128)(4,1)}), s8[1048576]{0:T(1024)(128)(4,1)S(1)}, s32[]{:S(2)}) async-start(s8[9437184]{0:T(1024)(128)(4,1)} %bitcast.114), calls=%async_computation.15 | async-start | bytes 2097152
  926.0 656.4 %copy-start.1 = (bf16[1024,256]{1,0:T(8,128)(2,1)S(1)}, bf16[1024,256]{1,0:T(8,128)(2,1)}, u32[]{:S(2)}) copy-start(bf16[1024,256]{1,0:T(8,128)(2,1)} %param.7) | copy-start | bytes 1572868
Sparse Core Ops, SparseCore 0:
  16.1 50.6 all-reduce.2
  945.3 637.0 reduce-scatter.1
